TPU v7x, 512 devices: a whole 4x8x8 slice. The times are simulated.
512 devices in a mesh: space: 32 (over y, z_lo), mode: 16 (over x, z_hi, core).
Axes of the slice: x: 4, y: 8, z: 8 (z_hi: 2, z_lo: 4; z = z_hi * 4 + z_lo), core: 2. Of those that a mesh axis runs over, the one named last changes fastest.
Arguments:
- old_modes: bfloat16 [512, 64, 4096], P('mode', None, 'space'), as said below
- new_modes: bfloat16 [512, 64, 4096], P('mode', None, 'space'), as said below
- material: int32 [64, 4096], P(None, 'space'), may hold values from 0 to 11
- density: float32 [12], replicated, may hold values from 0.5 to 2
- memb_x: bfloat16 [12], replicated, may hold values from 1 to 4
- memb_y: bfloat16 [12], replicated, may hold values from 1 to 4
- bend_table: float32 [12], replicated, may hold values from 0.02 to 0.1
Outputs:
- cross_mass: float32 [512, 512], P(None, 'mode')
- cross_membrane: float32 [512, 512], P(None, 'mode')
- cross_bending: float32 [512, 512], P(None, 'mode')
- mass_image: bfloat16 [512, 64, 4096], P('mode', None, 'space')
- stiff_image: bfloat16 [512, 64, 4096], P('mode', None, 'space')
Inputs may be any that keep to these rules, and one draw needn't show every extreme that they name: `old_modes`: A value of one mode shape at one cell. `new_modes`: A value of one mode shape at one cell.
All inputs are finite; a program needn't handle non-finite values.
Results may differ from a plain program's by a relative error of at most 0.0015.
Values may be sent and summed in bfloat16 or wider, within the bound.
No kernel may reach another device: no remote copies, remote signals or barrier semaphores. Data moves between devices by JAX's collectives and lax.ppermute only.
A program may use at most 64 MiB of HBM per device.

v0:
```python
import jax
import jax.numpy as jnp
from jax import lax
from jax.sharding import PartitionSpec as P


def extended(shard, sides, width):
    for axis, dim in sides:
        devices, length = (lax.axis_size(axis), shard.shape[dim])
        up = [(i, (i + 1) % devices) for i in range(devices - 1)]
        down = [(j, i) for i, j in up]
        last = lax.slice_in_dim(shard, length - width, length, axis=dim)
        initial = lax.slice_in_dim(shard, 0, width, axis=dim)
        before = lax.ppermute(last, axis, up)
        after = lax.ppermute(initial, axis, down)
        shard = jnp.concatenate([before, shard, after], axis=dim)
    return shard


def passed_along(value, axis, steps):
    count = lax.axis_size(axis)
    pairs = [(source, (source + steps) % count) for source in range(count)]
    return lax.ppermute(value, axis, pairs)


def lookup(material, table):
    levels = jnp.arange(table.shape[0], dtype=jnp.int32)
    picks = (material[None, :, :] == levels[:, None, None]).astype(jnp.float32)
    return jnp.sum(picks * table.astype(jnp.float32)[:, None, None], axis=0)


def operators(padded, kxp, kyp, density_field, bend_field, rows, cols):

    def moved(a, b):
        return padded[:, 2 + a : 2 + a + rows, 2 + b : 2 + b + cols]

    center = moved(0, 0)
    east = moved(1, 0)
    west = moved(-1, 0)
    north = moved(0, 1)
    south = moved(0, -1)
    nearest = east + west + north + south
    mass = density_field * (2.0 / 3.0 * center + nearest / 12.0)
    face_e = 0.5 * (kxp[1:-1, 1:-1] + kxp[2:, 1:-1])
    face_w = 0.5 * (kxp[1:-1, 1:-1] + kxp[:-2, 1:-1])
    face_n = 0.5 * (kyp[1:-1, 1:-1] + kyp[1:-1, 2:])
    face_s = 0.5 * (kyp[1:-1, 1:-1] + kyp[1:-1, :-2])
    membrane = (
        face_e * (center - east)
        + face_w * (center - west)
        + face_n * (center - north)
        + face_s * (center - south)
    )
    diagonals = moved(1, 1) + moved(1, -1) + moved(-1, 1) + moved(-1, -1)
    distant = moved(2, 0) + moved(-2, 0) + moved(0, 2) + moved(0, -2)
    bending = bend_field * (20.0 * center - 8.0 * nearest + 2.0 * diagonals + distant)
    return (mass, membrane, bending)


def local(old_modes, new_modes, material, density, memb_x, memb_y, bend_table):
    panel_size, rows, cols = new_modes.shape
    density_field = lookup(material, density)
    kxp = jnp.pad(lookup(material, memb_x), 1)
    ky_field = lookup(material, memb_y).astype(jnp.bfloat16)
    bend_field = lookup(material, bend_table)
    stacked = jnp.concatenate([new_modes, ky_field[None]], axis=0)
    rimmed = extended(stacked, (("space", 2),), 2)
    rimmed = jnp.pad(rimmed, ((0, 0), (2, 2), (0, 0)))
    padded = rimmed[:panel_size].astype(jnp.float32)
    kyp = rimmed[panel_size, 1:-1, 1:-1].astype(jnp.float32)
    mass, membrane, bending = operators(padded, kxp, kyp, density_field, bend_field, rows, cols)
    mass_image = mass.astype(jnp.bfloat16)
    stiff_image = (membrane + bending).astype(jnp.bfloat16)
    images = jnp.concatenate([mass, membrane, bending], axis=0).reshape(3 * panel_size, rows * cols)
    index = lax.axis_index("mode")
    loop_size = lax.axis_size("mode")
    area = 1.0 / (rows * cols * lax.axis_size("space"))

    def place(grams, panel, owner):
        block = lax.dot_general(
            panel.reshape(panel_size, rows * cols).astype(jnp.float32),
            images,
            (((1,), (1,)), ((), ())),
            precision=lax.Precision.HIGHEST,
            preferred_element_type=jnp.float32,
        )
        start = jnp.mod(owner, loop_size) * panel_size
        return lax.dynamic_update_slice(grams, block, (start, jnp.int32(0)))

    grams = jnp.zeros((loop_size * panel_size, 3 * panel_size), jnp.float32)
    grams = place(grams, old_modes, index)

    def turn(step, carry):
        panel, totals = carry
        panel = passed_along(panel, "mode", 1)
        return (panel, place(totals, panel, index - step))

    last, grams = lax.fori_loop(1, loop_size, turn, (old_modes, grams))
    total = lax.psum(grams, "space")
    cross_mass = total[:, :panel_size] * area
    cross_membrane = total[:, panel_size : 2 * panel_size] * area
    cross_bending = total[:, 2 * panel_size :] * area
    return (cross_mass, cross_membrane, cross_bending, mass_image, stiff_image)


def solution(mesh):
    in_specs = (
        P("mode", None, "space"),
        P("mode", None, "space"),
        P(None, "space"),
        P(),
        P(),
        P(),
        P(),
    )
    out_specs = (
        P(None, "mode"),
        P(None, "mode"),
        P(None, "mode"),
        P("mode", None, "space"),
        P("mode", None, "space"),
    )
    return jax.shard_map(local, mesh=mesh, in_specs=in_specs, out_specs=out_specs, check_vma=False)
```

profile of v0, /device:TPU:2, one launch (start us, length us, event | category | flops | bytes accessed | tf_op | source)
XLA Modules:
  0.0 738.0 jit_solution(993492930398526759)
XLA Ops:
  13.9 4.9 collective-permute-start.1
  24.7 7.6 %add_convert_fusion = (bf16[32,64,128]{1,0,2:T(8,128)(2,1)}, f32[32,64,128]{1,0,2:T(8,128)S(1)}, f32[32,64,128]{1,0,2:T(8,128)S(1)}, f32[32,64,128]{1,0,2:T(8,128)S(1)}) fusion(f32[32,68,132]{1,0,2:T(8,128)S(1)} %slice_convert_fusion, f32[64,128]{0,1:T(8,128)S(1)} %copy.93, f32[64,128]{0,1:T(8,128)S(1)} %copy.91, f32[64,128]{0,1:T(8,128)S(1)} %copy.88, ...), kind=kLoop, calls=%fused_computation.18 | loop fusion | flops 7602176 | bytes 17465344 | tf_op jit(solution)/shard_map/convert_element_type | solution.py:73
  35.9 3.3 pad_maximum_fusion
  39.2 6.8 copy.97
  46.0 4.3 copy.112
  50.3 5.5 fusion.12
  55.8 336.8 %while.17 = (s32[]{:T(128)}, bf16[32,64,128]{2,1,0:T(8,128)(2,1)}, f32[512,96]{1,0:T(8,128)S(1)}, f32[96,8192]{1,0:T(8,128)S(1)}, s32[]{:T(128)}, /*index=5*/s32...) while((s32[]{:T(128)}, bf16[32,64,128]{2,1,0:T(8,128)(2,1)}, ...), condition=%wide.region_5.6_spmd, body=%wide.region_4.5_spmd.sunk | while | flops 301989920 | bytes 6832448 | solution.py:98
  57.8 14.7 %collective-permute-done = bf16[32,64,128]{2,1,0:T(8,128)(2,1)} collective-permute-done((bf16[32,64,128]{2,1,0:T(8,128)(2,1)}, bf16[32,64,128]{2,1,0:T(8,128)(2,1)}, u32[]{:S(2)}, u32[]{:S(2)}) %collective-permute-start) | collective-permute-done | bytes 524320 | tf_op jit(solution)/shard_map/while/body/eval_jaxpr/ppermute | solution.py:23
  77.2 7.9 %collective-permute-start = (bf16[32,64,128]{2,1,0:T(8,128)(2,1)}, bf16[32,64,128]{2,1,0:T(8,128)(2,1)}, u32[]{:S(2)}, u32[]{:S(2)}) collective-permute-start(bf16[32,64,128]{2,1,0:T(8,128)(2,1)} %get-tuple-element.241), channel_id=1, source_target_pairs={{0,1},{1,2},{2,3},{3,4},{4,5},{5,6},{6,7},{7,8},{8,9},{9,10},{10,1... | collective-permute-start | bytes 1572872 | tf_op jit(solution)/shard_map/while/body/eval_jaxpr/ppermute | solution.py:23
  85.1 7.6 %collective-permute-done = bf16[32,64,128]{2,1,0:T(8,128)(2,1)} collective-permute-done((bf16[32,64,128]{2,1,0:T(8,128)(2,1)}, bf16[32,64,128]{2,1,0:T(8,128)(2,1)}, u32[]{:S(2)}, u32[]{:S(2)}) %collective-permute-start) | collective-permute-done | bytes 524320 | tf_op jit(solution)/shard_map/while/body/eval_jaxpr/ppermute | solution.py:23
  92.8 2.8 convolution_dynamic-update-slice_fusion.2
  97.4 12.3 %collective-permute-start = (bf16[32,64,128]{2,1,0:T(8,128)(2,1)}, bf16[32,64,128]{2,1,0:T(8,128)(2,1)}, u32[]{:S(2)}, u32[]{:S(2)}) collective-permute-start(bf16[32,64,128]{2,1,0:T(8,128)(2,1)} %get-tuple-element.241), channel_id=1, source_target_pairs={{0,1},{1,2},{2,3},{3,4},{4,5},{5,6},{6,7},{7,8},{8,9},{9,10},{10,1... | collective-permute-start | bytes 1572872 | tf_op jit(solution)/shard_map/while/body/eval_jaxpr/ppermute | solution.py:23
  109.8 3.3 collective-permute-done
  113.0 2.8 convolution_dynamic-update-slice_fusion.2
  117.7 12.4 %collective-permute-start = (bf16[32,64,128]{2,1,0:T(8,128)(2,1)}, bf16[32,64,128]{2,1,0:T(8,128)(2,1)}, u32[]{:S(2)}, u32[]{:S(2)}) collective-permute-start(bf16[32,64,128]{2,1,0:T(8,128)(2,1)} %get-tuple-element.241), channel_id=1, source_target_pairs={{0,1},{1,2},{2,3},{3,4},{4,5},{5,6},{6,7},{7,8},{8,9},{9,10},{10,1... | collective-permute-start | bytes 1572872 | tf_op jit(solution)/shard_map/while/body/eval_jaxpr/ppermute | solution.py:23
  130.1 3.2 collective-permute-done
  133.3 2.8 convolution_dynamic-update-slice_fusion.2
  137.9 12.5 %collective-permute-start = (bf16[32,64,128]{2,1,0:T(8,128)(2,1)}, bf16[32,64,128]{2,1,0:T(8,128)(2,1)}, u32[]{:S(2)}, u32[]{:S(2)}) collective-permute-start(bf16[32,64,128]{2,1,0:T(8,128)(2,1)} %get-tuple-element.241), channel_id=1, source_target_pairs={{0,1},{1,2},{2,3},{3,4},{4,5},{5,6},{6,7},{7,8},{8,9},{9,10},{10,1... | collective-permute-start | bytes 1572872 | tf_op jit(solution)/shard_map/while/body/eval_jaxpr/ppermute | solution.py:23
  150.5 3.1 collective-permute-done
  153.6 2.8 convolution_dynamic-update-slice_fusion.2
  158.2 12.6 %collective-permute-start = (bf16[32,64,128]{2,1,0:T(8,128)(2,1)}, bf16[32,64,128]{2,1,0:T(8,128)(2,1)}, u32[]{:S(2)}, u32[]{:S(2)}) collective-permute-start(bf16[32,64,128]{2,1,0:T(8,128)(2,1)} %get-tuple-element.241), channel_id=1, source_target_pairs={{0,1},{1,2},{2,3},{3,4},{4,5},{5,6},{6,7},{7,8},{8,9},{9,10},{10,1... | collective-permute-start | bytes 1572872 | tf_op jit(solution)/shard_map/while/body/eval_jaxpr/ppermute | solution.py:23
  170.8 3.0 collective-permute-done
  173.8 2.8 convolution_dynamic-update-slice_fusion.2
  178.5 12.7 %collective-permute-start = (bf16[32,64,128]{2,1,0:T(8,128)(2,1)}, bf16[32,64,128]{2,1,0:T(8,128)(2,1)}, u32[]{:S(2)}, u32[]{:S(2)}) collective-permute-start(bf16[32,64,128]{2,1,0:T(8,128)(2,1)} %get-tuple-element.241), channel_id=1, source_target_pairs={{0,1},{1,2},{2,3},{3,4},{4,5},{5,6},{6,7},{7,8},{8,9},{9,10},{10,1... | collective-permute-start | bytes 1572872 | tf_op jit(solution)/shard_map/while/body/eval_jaxpr/ppermute | solution.py:23
  191.2 2.9 collective-permute-done
  194.1 2.8 convolution_dynamic-update-slice_fusion.2
  198.7 12.8 %collective-permute-start = (bf16[32,64,128]{2,1,0:T(8,128)(2,1)}, bf16[32,64,128]{2,1,0:T(8,128)(2,1)}, u32[]{:S(2)}, u32[]{:S(2)}) collective-permute-start(bf16[32,64,128]{2,1,0:T(8,128)(2,1)} %get-tuple-element.241), channel_id=1, source_target_pairs={{0,1},{1,2},{2,3},{3,4},{4,5},{5,6},{6,7},{7,8},{8,9},{9,10},{10,1... | collective-permute-start | bytes 1572872 | tf_op jit(solution)/shard_map/while/body/eval_jaxpr/ppermute | solution.py:23
  211.5 3.3 collective-permute-done
  214.9 2.8 convolution_dynamic-update-slice_fusion.2
  219.6 13.3 %collective-permute-start = (bf16[32,64,128]{2,1,0:T(8,128)(2,1)}, bf16[32,64,128]{2,1,0:T(8,128)(2,1)}, u32[]{:S(2)}, u32[]{:S(2)}) collective-permute-start(bf16[32,64,128]{2,1,0:T(8,128)(2,1)} %get-tuple-element.241), channel_id=1, source_target_pairs={{0,1},{1,2},{2,3},{3,4},{4,5},{5,6},{6,7},{7,8},{8,9},{9,10},{10,1... | collective-permute-start | bytes 1572872 | tf_op jit(solution)/shard_map/while/body/eval_jaxpr/ppermute | solution.py:23
  232.9 7.6 %collective-permute-done = bf16[32,64,128]{2,1,0:T(8,128)(2,1)} collective-permute-done((bf16[32,64,128]{2,1,0:T(8,128)(2,1)}, bf16[32,64,128]{2,1,0:T(8,128)(2,1)}, u32[]{:S(2)}, u32[]{:S(2)}) %collective-permute-start) | collective-permute-done | bytes 524320 | tf_op jit(solution)/shard_map/while/body/eval_jaxpr/ppermute | solution.py:23
  245.1 12.7 %collective-permute-start = (bf16[32,64,128]{2,1,0:T(8,128)(2,1)}, bf16[32,64,128]{2,1,0:T(8,128)(2,1)}, u32[]{:S(2)}, u32[]{:S(2)}) collective-permute-start(bf16[32,64,128]{2,1,0:T(8,128)(2,1)} %get-tuple-element.241), channel_id=1, source_target_pairs={{0,1},{1,2},{2,3},{3,4},{4,5},{5,6},{6,7},{7,8},{8,9},{9,10},{10,1... | collective-permute-start | bytes 1572872 | tf_op jit(solution)/shard_map/while/body/eval_jaxpr/ppermute | solution.py:23
  257.8 8.4 %collective-permute-done = bf16[32,64,128]{2,1,0:T(8,128)(2,1)} collective-permute-done((bf16[32,64,128]{2,1,0:T(8,128)(2,1)}, bf16[32,64,128]{2,1,0:T(8,128)(2,1)}, u32[]{:S(2)}, u32[]{:S(2)}) %collective-permute-start) | collective-permute-done | bytes 524320 | tf_op jit(solution)/shard_map/while/body/eval_jaxpr/ppermute | solution.py:23
  270.9 11.1 %collective-permute-start = (bf16[32,64,128]{2,1,0:T(8,128)(2,1)}, bf16[32,64,128]{2,1,0:T(8,128)(2,1)}, u32[]{:S(2)}, u32[]{:S(2)}) collective-permute-start(bf16[32,64,128]{2,1,0:T(8,128)(2,1)} %get-tuple-element.241), channel_id=1, source_target_pairs={{0,1},{1,2},{2,3},{3,4},{4,5},{5,6},{6,7},{7,8},{8,9},{9,10},{10,1... | collective-permute-start | bytes 1572872 | tf_op jit(solution)/shard_map/while/body/eval_jaxpr/ppermute | solution.py:23
  282.0 6.9 collective-permute-done
  293.5 11.7 %collective-permute-start = (bf16[32,64,128]{2,1,0:T(8,128)(2,1)}, bf16[32,64,128]{2,1,0:T(8,128)(2,1)}, u32[]{:S(2)}, u32[]{:S(2)}) collective-permute-start(bf16[32,64,128]{2,1,0:T(8,128)(2,1)} %get-tuple-element.241), channel_id=1, source_target_pairs={{0,1},{1,2},{2,3},{3,4},{4,5},{5,6},{6,7},{7,8},{8,9},{9,10},{10,1... | collective-permute-start | bytes 1572872 | tf_op jit(solution)/shard_map/while/body/eval_jaxpr/ppermute | solution.py:23
  305.3 7.3 collective-permute-done
  312.6 2.8 convolution_dynamic-update-slice_fusion.2
  317.3 12.3 %collective-permute-start = (bf16[32,64,128]{2,1,0:T(8,128)(2,1)}, bf16[32,64,128]{2,1,0:T(8,128)(2,1)}, u32[]{:S(2)}, u32[]{:S(2)}) collective-permute-start(bf16[32,64,128]{2,1,0:T(8,128)(2,1)} %get-tuple-element.241), channel_id=1, source_target_pairs={{0,1},{1,2},{2,3},{3,4},{4,5},{5,6},{6,7},{7,8},{8,9},{9,10},{10,1... | collective-permute-start | bytes 1572872 | tf_op jit(solution)/shard_map/while/body/eval_jaxpr/ppermute | solution.py:23
  329.6 8.0 %collective-permute-done = bf16[32,64,128]{2,1,0:T(8,128)(2,1)} collective-permute-done((bf16[32,64,128]{2,1,0:T(8,128)(2,1)}, bf16[32,64,128]{2,1,0:T(8,128)(2,1)}, u32[]{:S(2)}, u32[]{:S(2)}) %collective-permute-start) | collective-permute-done | bytes 524320 | tf_op jit(solution)/shard_map/while/body/eval_jaxpr/ppermute | solution.py:23
  342.3 11.3 %collective-permute-start = (bf16[32,64,128]{2,1,0:T(8,128)(2,1)}, bf16[32,64,128]{2,1,0:T(8,128)(2,1)}, u32[]{:S(2)}, u32[]{:S(2)}) collective-permute-start(bf16[32,64,128]{2,1,0:T(8,128)(2,1)} %get-tuple-element.241), channel_id=1, source_target_pairs={{0,1},{1,2},{2,3},{3,4},{4,5},{5,6},{6,7},{7,8},{8,9},{9,10},{10,1... | collective-permute-start | bytes 1572872 | tf_op jit(solution)/shard_map/while/body/eval_jaxpr/ppermute | solution.py:23
  353.6 9.6 %collective-permute-done = bf16[32,64,128]{2,1,0:T(8,128)(2,1)} collective-permute-done((bf16[32,64,128]{2,1,0:T(8,128)(2,1)}, bf16[32,64,128]{2,1,0:T(8,128)(2,1)}, u32[]{:S(2)}, u32[]{:S(2)}) %collective-permute-start) | collective-permute-done | bytes 524320 | tf_op jit(solution)/shard_map/while/body/eval_jaxpr/ppermute | solution.py:23
  363.2 2.8 convolution_dynamic-update-slice_fusion.2
  367.9 10.7 %collective-permute-start = (bf16[32,64,128]{2,1,0:T(8,128)(2,1)}, bf16[32,64,128]{2,1,0:T(8,128)(2,1)}, u32[]{:S(2)}, u32[]{:S(2)}) collective-permute-start(bf16[32,64,128]{2,1,0:T(8,128)(2,1)} %get-tuple-element.241), channel_id=1, source_target_pairs={{0,1},{1,2},{2,3},{3,4},{4,5},{5,6},{6,7},{7,8},{8,9},{9,10},{10,1... | collective-permute-start | bytes 1572872 | tf_op jit(solution)/shard_map/while/body/eval_jaxpr/ppermute | solution.py:23
  378.6 9.4 %collective-permute-done = bf16[32,64,128]{2,1,0:T(8,128)(2,1)} collective-permute-done((bf16[32,64,128]{2,1,0:T(8,128)(2,1)}, bf16[32,64,128]{2,1,0:T(8,128)(2,1)}, u32[]{:S(2)}, u32[]{:S(2)}) %collective-permute-start) | collective-permute-done | bytes 524320 | tf_op jit(solution)/shard_map/while/body/eval_jaxpr/ppermute | solution.py:23
  388.0 2.8 convolution_dynamic-update-slice_fusion.2
  393.5 3.0 copy.100
  398.4 331.2 %all-reduce.4.cloned.1.call-done = f32[512,96]{0,1:T(8,128)} async-done(((f32[512,96]{0,1:T(8,128)}), f32[512,96]{0,1:T(8,128)}) %all-reduce.4.cloned.1.call-update) | async-done | bytes 196624 | tf_op jit(solution)/shard_map/psum | solution.py:99
  (73 shorter events, 64.1 us)
Async XLA Ops:
  7.2 11.7 %copy-start.7 = (bf16[32,64,128]{2,1,0:T(8,128)(2,1)S(1)}, bf16[32,64,128]{2,1,0:T(8,128)(2,1)}, u32[]{:S(2)}) copy-start(bf16[32,64,128]{2,1,0:T(8,128)(2,1)} %param.10) | copy-start | bytes 1572868
  7.2 722.4 %all-reduce.4.cloned.1.call-start = ((), (), s32[]{:S(2)}) async-start(), calls=%async_computation | async-start | bytes 393216 | tf_op jit(solution)/shard_map/psum | solution.py:99
  8.3 12.2 %copy-start.8 = (bf16[32,64,128]{2,1,0:T(8,128)(2,1)}, bf16[32,64,128]{2,1,0:T(8,128)(2,1)S(1)}, u32[]{:S(2)}) copy-start(bf16[32,64,128]{2,1,0:T(8,128)(2,1)S(1)} %copy.128) | copy-start | bytes 1572868
  12.3 10.8 %collective-permute-start.2 = (bf16[33,64,2]{1,2,0:T(2,128)(2,1)S(1)}, bf16[33,64,2]{1,2,0:T(2,128)(2,1)S(1)}, u32[]{:S(2)}, u32[]{:S(2)}) collective-permute-start(bf16[33,64,2]{1,2,0:T(2,128)(2,1)S(1)} %copy.104), channel_id=1, source_target_pairs={{16,0},{32,16},{48,32},{64,48},{80,64},{96,80},{112,96},{128,112},... | collective-permute-start | bytes 25352 | tf_op jit(solution)/shard_map/ppermute | solution.py:15
  13.9 9.2 %collective-permute-start.1 = (bf16[33,64,2]{1,2,0:T(2,128)(2,1)S(1)}, bf16[33,64,2]{1,2,0:T(2,128)(2,1)S(1)}, u32[]{:S(2)}, u32[]{:S(2)}) collective-permute-start(bf16[33,64,2]{1,2,0:T(2,128)(2,1)S(1)} %copy.103), channel_id=1, source_target_pairs={{0,16},{16,32},{32,48},{48,64},{64,80},{80,96},{96,112},{112,128},... | collective-permute-start | bytes 25352 | tf_op jit(solution)/shard_map/ppermute | solution.py:14
  32.3 2.2 copy-start
  32.3 2.4 copy-start.2
  34.6 1.3 copy-start.4
  46.0 4.3 copy-start.1
  46.0 4.3 copy-start.3
  46.0 4.3 copy-start.5
  55.8 16.7 %collective-permute-start = (bf16[32,64,128]{2,1,0:T(8,128)(2,1)}, bf16[32,64,128]{2,1,0:T(8,128)(2,1)}, u32[]{:S(2)}, u32[]{:S(2)}) collective-permute-start(bf16[32,64,128]{2,1,0:T(8,128)(2,1)} %get-tuple-element.241), channel_id=1, source_target_pairs={{0,1},{1,2},{2,3},{3,4},{4,5},{5,6},{6,7},{7,8},{8,9},{9,10},{10,1... | collective-permute-start | bytes 1572872 | tf_op jit(solution)/shard_map/while/body/eval_jaxpr/ppermute | solution.py:23
  77.2 15.6 %collective-permute-start = (bf16[32,64,128]{2,1,0:T(8,128)(2,1)}, bf16[32,64,128]{2,1,0:T(8,128)(2,1)}, u32[]{:S(2)}, u32[]{:S(2)}) collective-permute-start(bf16[32,64,128]{2,1,0:T(8,128)(2,1)} %get-tuple-element.241), channel_id=1, source_target_pairs={{0,1},{1,2},{2,3},{3,4},{4,5},{5,6},{6,7},{7,8},{8,9},{9,10},{10,1... | collective-permute-start | bytes 1572872 | tf_op jit(solution)/shard_map/while/body/eval_jaxpr/ppermute | solution.py:23
  97.4 15.6 %collective-permute-start = (bf16[32,64,128]{2,1,0:T(8,128)(2,1)}, bf16[32,64,128]{2,1,0:T(8,128)(2,1)}, u32[]{:S(2)}, u32[]{:S(2)}) collective-permute-start(bf16[32,64,128]{2,1,0:T(8,128)(2,1)} %get-tuple-element.241), channel_id=1, source_target_pairs={{0,1},{1,2},{2,3},{3,4},{4,5},{5,6},{6,7},{7,8},{8,9},{9,10},{10,1... | collective-permute-start | bytes 1572872 | tf_op jit(solution)/shard_map/while/body/eval_jaxpr/ppermute | solution.py:23
  117.7 15.6 %collective-permute-start = (bf16[32,64,128]{2,1,0:T(8,128)(2,1)}, bf16[32,64,128]{2,1,0:T(8,128)(2,1)}, u32[]{:S(2)}, u32[]{:S(2)}) collective-permute-start(bf16[32,64,128]{2,1,0:T(8,128)(2,1)} %get-tuple-element.241), channel_id=1, source_target_pairs={{0,1},{1,2},{2,3},{3,4},{4,5},{5,6},{6,7},{7,8},{8,9},{9,10},{10,1... | collective-permute-start | bytes 1572872 | tf_op jit(solution)/shard_map/while/body/eval_jaxpr/ppermute | solution.py:23
  137.9 15.6 %collective-permute-start = (bf16[32,64,128]{2,1,0:T(8,128)(2,1)}, bf16[32,64,128]{2,1,0:T(8,128)(2,1)}, u32[]{:S(2)}, u32[]{:S(2)}) collective-permute-start(bf16[32,64,128]{2,1,0:T(8,128)(2,1)} %get-tuple-element.241), channel_id=1, source_target_pairs={{0,1},{1,2},{2,3},{3,4},{4,5},{5,6},{6,7},{7,8},{8,9},{9,10},{10,1... | collective-permute-start | bytes 1572872 | tf_op jit(solution)/shard_map/while/body/eval_jaxpr/ppermute | solution.py:23
  158.2 15.6 %collective-permute-start = (bf16[32,64,128]{2,1,0:T(8,128)(2,1)}, bf16[32,64,128]{2,1,0:T(8,128)(2,1)}, u32[]{:S(2)}, u32[]{:S(2)}) collective-permute-start(bf16[32,64,128]{2,1,0:T(8,128)(2,1)} %get-tuple-element.241), channel_id=1, source_target_pairs={{0,1},{1,2},{2,3},{3,4},{4,5},{5,6},{6,7},{7,8},{8,9},{9,10},{10,1... | collective-permute-start | bytes 1572872 | tf_op jit(solution)/shard_map/while/body/eval_jaxpr/ppermute | solution.py:23
  178.5 15.6 %collective-permute-start = (bf16[32,64,128]{2,1,0:T(8,128)(2,1)}, bf16[32,64,128]{2,1,0:T(8,128)(2,1)}, u32[]{:S(2)}, u32[]{:S(2)}) collective-permute-start(bf16[32,64,128]{2,1,0:T(8,128)(2,1)} %get-tuple-element.241), channel_id=1, source_target_pairs={{0,1},{1,2},{2,3},{3,4},{4,5},{5,6},{6,7},{7,8},{8,9},{9,10},{10,1... | collective-permute-start | bytes 1572872 | tf_op jit(solution)/shard_map/while/body/eval_jaxpr/ppermute | solution.py:23
  198.7 16.1 %collective-permute-start = (bf16[32,64,128]{2,1,0:T(8,128)(2,1)}, bf16[32,64,128]{2,1,0:T(8,128)(2,1)}, u32[]{:S(2)}, u32[]{:S(2)}) collective-permute-start(bf16[32,64,128]{2,1,0:T(8,128)(2,1)} %get-tuple-element.241), channel_id=1, source_target_pairs={{0,1},{1,2},{2,3},{3,4},{4,5},{5,6},{6,7},{7,8},{8,9},{9,10},{10,1... | collective-permute-start | bytes 1572872 | tf_op jit(solution)/shard_map/while/body/eval_jaxpr/ppermute | solution.py:23
  219.6 20.9 %collective-permute-start = (bf16[32,64,128]{2,1,0:T(8,128)(2,1)}, bf16[32,64,128]{2,1,0:T(8,128)(2,1)}, u32[]{:S(2)}, u32[]{:S(2)}) collective-permute-start(bf16[32,64,128]{2,1,0:T(8,128)(2,1)} %get-tuple-element.241), channel_id=1, source_target_pairs={{0,1},{1,2},{2,3},{3,4},{4,5},{5,6},{6,7},{7,8},{8,9},{9,10},{10,1... | collective-permute-start | bytes 1572872 | tf_op jit(solution)/shard_map/while/body/eval_jaxpr/ppermute | solution.py:23
  245.1 21.1 %collective-permute-start = (bf16[32,64,128]{2,1,0:T(8,128)(2,1)}, bf16[32,64,128]{2,1,0:T(8,128)(2,1)}, u32[]{:S(2)}, u32[]{:S(2)}) collective-permute-start(bf16[32,64,128]{2,1,0:T(8,128)(2,1)} %get-tuple-element.241), channel_id=1, source_target_pairs={{0,1},{1,2},{2,3},{3,4},{4,5},{5,6},{6,7},{7,8},{8,9},{9,10},{10,1... | collective-permute-start | bytes 1572872 | tf_op jit(solution)/shard_map/while/body/eval_jaxpr/ppermute | solution.py:23
  270.9 18.0 %collective-permute-start = (bf16[32,64,128]{2,1,0:T(8,128)(2,1)}, bf16[32,64,128]{2,1,0:T(8,128)(2,1)}, u32[]{:S(2)}, u32[]{:S(2)}) collective-permute-start(bf16[32,64,128]{2,1,0:T(8,128)(2,1)} %get-tuple-element.241), channel_id=1, source_target_pairs={{0,1},{1,2},{2,3},{3,4},{4,5},{5,6},{6,7},{7,8},{8,9},{9,10},{10,1... | collective-permute-start | bytes 1572872 | tf_op jit(solution)/shard_map/while/body/eval_jaxpr/ppermute | solution.py:23
  293.5 19.1 %collective-permute-start = (bf16[32,64,128]{2,1,0:T(8,128)(2,1)}, bf16[32,64,128]{2,1,0:T(8,128)(2,1)}, u32[]{:S(2)}, u32[]{:S(2)}) collective-permute-start(bf16[32,64,128]{2,1,0:T(8,128)(2,1)} %get-tuple-element.241), channel_id=1, source_target_pairs={{0,1},{1,2},{2,3},{3,4},{4,5},{5,6},{6,7},{7,8},{8,9},{9,10},{10,1... | collective-permute-start | bytes 1572872 | tf_op jit(solution)/shard_map/while/body/eval_jaxpr/ppermute | solution.py:23
  317.3 20.4 %collective-permute-start = (bf16[32,64,128]{2,1,0:T(8,128)(2,1)}, bf16[32,64,128]{2,1,0:T(8,128)(2,1)}, u32[]{:S(2)}, u32[]{:S(2)}) collective-permute-start(bf16[32,64,128]{2,1,0:T(8,128)(2,1)} %get-tuple-element.241), channel_id=1, source_target_pairs={{0,1},{1,2},{2,3},{3,4},{4,5},{5,6},{6,7},{7,8},{8,9},{9,10},{10,1... | collective-permute-start | bytes 1572872 | tf_op jit(solution)/shard_map/while/body/eval_jaxpr/ppermute | solution.py:23
  342.3 20.9 %collective-permute-start = (bf16[32,64,128]{2,1,0:T(8,128)(2,1)}, bf16[32,64,128]{2,1,0:T(8,128)(2,1)}, u32[]{:S(2)}, u32[]{:S(2)}) collective-permute-start(bf16[32,64,128]{2,1,0:T(8,128)(2,1)} %get-tuple-element.241), channel_id=1, source_target_pairs={{0,1},{1,2},{2,3},{3,4},{4,5},{5,6},{6,7},{7,8},{8,9},{9,10},{10,1... | collective-permute-start | bytes 1572872 | tf_op jit(solution)/shard_map/while/body/eval_jaxpr/ppermute | solution.py:23
  367.9 20.1 %collective-permute-start = (bf16[32,64,128]{2,1,0:T(8,128)(2,1)}, bf16[32,64,128]{2,1,0:T(8,128)(2,1)}, u32[]{:S(2)}, u32[]{:S(2)}) collective-permute-start(bf16[32,64,128]{2,1,0:T(8,128)(2,1)} %get-tuple-element.241), channel_id=1, source_target_pairs={{0,1},{1,2},{2,3},{3,4},{4,5},{5,6},{6,7},{7,8},{8,9},{9,10},{10,1... | collective-permute-start | bytes 1572872 | tf_op jit(solution)/shard_map/while/body/eval_jaxpr/ppermute | solution.py:23
  392.7 3.8 copy-start.6
Sparse Core Ops, SparseCore 0:
  393.6 335.9 all-reduce.3
where the time goes:
time: 740 us; the launch traced here: 738 us
  waiting for transfers between devices  430 us (58%)
  starting transfers between devices  174 us (24%)
  local copies, waits for them, and re-layouts  52.2 us (7%)
  matrix products  47.1 us (6%)
  other arithmetic  19.8 us (3%)
  between operations  14.3 us (2%)
    psum x1, waiting for transfers between devices, local(): total = lax.psum(grams, 'space')  331 us
    ppermute x15, starting transfers between devices, passed_along(): return lax.ppermute(value, axis, pairs)  168 us
    ppermute x15, waiting for transfers between devices, passed_along(): return lax.ppermute(value, axis, pairs)  98.3 us
    dot_general x16, matrix products, place(): lax.dot_general(panel.reshape(panel_size, rows * cols).astype(jnp.float32...  47.1 us
    while x15, local copies, waits for them, and re-layouts  28 us
  transfers between devices with their start and end apart: 18, of which 16 were waited for; matrix products, arithmetic and copies ran while one was open for 1% of the time, Pallas kernels for 0%

commit v1 on v0

--- a/solution.py
+++ b/solution.py
@@ -96,7 +96,7 @@
         return (panel, place(totals, panel, index - step))
 
     last, grams = lax.fori_loop(1, loop_size, turn, (old_modes, grams))
-    total = lax.psum(grams, "space")
+    total = jnp.sum(lax.all_gather(grams, axis_name="space"), 0)
     cross_mass = total[:, :panel_size] * area
     cross_membrane = total[:, panel_size : 2 * panel_size] * area
     cross_bending = total[:, 2 * panel_size :] * area

time: 740 us -> 642 us (0.87)
  the two profiles are of different devices: /device:TPU:2 before, /device:TPU:4 now
where the time goes in v1:
time: 642 us; the launch traced here: 640 us
  waiting for transfers between devices  348 us (54%)
  starting transfers between devices  153 us (24%)
  local copies, waits for them, and re-layouts  54.4 us (8%)
  matrix products  47.1 us (7%)
  other arithmetic  22.4 us (3%)
  between operations  14.3 us (2%)
    all_gather x1, waiting for transfers between devices, local(): total = jnp.sum(lax.all_gather(grams, axis_name='space'), 0)  229 us
    ppermute x15, starting transfers between devices, passed_along(): return lax.ppermute(value, axis, pairs)  147 us
    ppermute x15, waiting for transfers between devices, passed_along(): return lax.ppermute(value, axis, pairs)  118 us
    dot_general x16, matrix products, place(): lax.dot_general(panel.reshape(panel_size, rows * cols).astype(jnp.float32...  47.1 us
    while x15, local copies, waits for them, and re-layouts  28 us
    unnamed x30, local copies, waits for them, and re-layouts  17.6 us
  transfers between devices with their start and end apart: 18, of which 16 were waited for; matrix products, arithmetic and copies ran while one was open for 1% of the time, Pallas kernels for 0%

profile of v1, /device:TPU:4, one launch (start us, length us, event | category | flops | bytes accessed | tf_op | source)
XLA Modules:
  0.0 639.5 jit_solution(9209838769536693478)
XLA Ops:
  13.9 4.9 collective-permute-start.1
  24.7 7.6 %add_convert_fusion = (bf16[32,64,128]{1,0,2:T(8,128)(2,1)}, f32[32,64,128]{1,0,2:T(8,128)S(1)}, f32[32,64,128]{1,0,2:T(8,128)S(1)}, f32[32,64,128]{1,0,2:T(8,128)S(1)}) fusion(f32[32,68,132]{1,0,2:T(8,128)S(1)} %slice_convert_fusion, f32[64,128]{0,1:T(8,128)S(1)} %copy.97, f32[64,128]{0,1:T(8,128)S(1)} %copy.95, f32[64,128]{0,1:T(8,128)S(1)} %copy.92, ...), kind=kLoop, calls=%fused_computation.18 | loop fusion | flops 7602176 | bytes 17465344 | tf_op jit(solution)/shard_map/convert_element_type | solution.py:73
  35.9 3.3 pad_maximum_fusion
  39.2 6.8 %copy.101 = f32[96,64,128]{2,1,0:T(8,128)} copy(f32[96,64,128]{1,0,2:T(8,128)} %pad_maximum_fusion) | data formatting | bytes 6291456 | tf_op jit(solution)/shard_map/concatenate | solution.py:74
  46.0 4.3 copy.118
  50.3 5.5 fusion.12
  55.8 335.4 %while.17 = (s32[]{:T(128)}, bf16[32,64,128]{2,1,0:T(8,128)(2,1)}, f32[512,96]{1,0:T(8,128)S(1)}, f32[96,8192]{1,0:T(8,128)S(1)}, s32[]{:T(128)}, /*index=5*/s32...) while((s32[]{:T(128)}, bf16[32,64,128]{2,1,0:T(8,128)(2,1)}, ...), condition=%wide.region_5.6_spmd, body=%wide.region_4.5_spmd.sunk | while | flops 301989920 | bytes 6832448 | solution.py:98
  57.8 14.7 %collective-permute-done = bf16[32,64,128]{2,1,0:T(8,128)(2,1)} collective-permute-done((bf16[32,64,128]{2,1,0:T(8,128)(2,1)}, bf16[32,64,128]{2,1,0:T(8,128)(2,1)}, u32[]{:S(2)}, u32[]{:S(2)}) %collective-permute-start) | collective-permute-done | bytes 524320 | tf_op jit(solution)/shard_map/while/body/eval_jaxpr/ppermute | solution.py:23
  77.1 7.9 %collective-permute-start = (bf16[32,64,128]{2,1,0:T(8,128)(2,1)}, bf16[32,64,128]{2,1,0:T(8,128)(2,1)}, u32[]{:S(2)}, u32[]{:S(2)}) collective-permute-start(bf16[32,64,128]{2,1,0:T(8,128)(2,1)} %get-tuple-element.241), channel_id=1, source_target_pairs={{0,1},{1,2},{2,3},{3,4},{4,5},{5,6},{6,7},{7,8},{8,9},{9,10},{10,1... | collective-permute-start | bytes 1572872 | tf_op jit(solution)/shard_map/while/body/eval_jaxpr/ppermute | solution.py:23
  85.0 7.7 %collective-permute-done = bf16[32,64,128]{2,1,0:T(8,128)(2,1)} collective-permute-done((bf16[32,64,128]{2,1,0:T(8,128)(2,1)}, bf16[32,64,128]{2,1,0:T(8,128)(2,1)}, u32[]{:S(2)}, u32[]{:S(2)}) %collective-permute-start) | collective-permute-done | bytes 524320 | tf_op jit(solution)/shard_map/while/body/eval_jaxpr/ppermute | solution.py:23
  92.8 2.8 convolution_dynamic-update-slice_fusion.2
  97.4 12.3 %collective-permute-start = (bf16[32,64,128]{2,1,0:T(8,128)(2,1)}, bf16[32,64,128]{2,1,0:T(8,128)(2,1)}, u32[]{:S(2)}, u32[]{:S(2)}) collective-permute-start(bf16[32,64,128]{2,1,0:T(8,128)(2,1)} %get-tuple-element.241), channel_id=1, source_target_pairs={{0,1},{1,2},{2,3},{3,4},{4,5},{5,6},{6,7},{7,8},{8,9},{9,10},{10,1... | collective-permute-start | bytes 1572872 | tf_op jit(solution)/shard_map/while/body/eval_jaxpr/ppermute | solution.py:23
  109.7 3.3 collective-permute-done
  113.0 2.8 convolution_dynamic-update-slice_fusion.2
  117.7 12.4 %collective-permute-start = (bf16[32,64,128]{2,1,0:T(8,128)(2,1)}, bf16[32,64,128]{2,1,0:T(8,128)(2,1)}, u32[]{:S(2)}, u32[]{:S(2)}) collective-permute-start(bf16[32,64,128]{2,1,0:T(8,128)(2,1)} %get-tuple-element.241), channel_id=1, source_target_pairs={{0,1},{1,2},{2,3},{3,4},{4,5},{5,6},{6,7},{7,8},{8,9},{9,10},{10,1... | collective-permute-start | bytes 1572872 | tf_op jit(solution)/shard_map/while/body/eval_jaxpr/ppermute | solution.py:23
  130.1 3.2 collective-permute-done
  133.3 2.8 convolution_dynamic-update-slice_fusion.2
  137.9 12.5 %collective-permute-start = (bf16[32,64,128]{2,1,0:T(8,128)(2,1)}, bf16[32,64,128]{2,1,0:T(8,128)(2,1)}, u32[]{:S(2)}, u32[]{:S(2)}) collective-permute-start(bf16[32,64,128]{2,1,0:T(8,128)(2,1)} %get-tuple-element.241), channel_id=1, source_target_pairs={{0,1},{1,2},{2,3},{3,4},{4,5},{5,6},{6,7},{7,8},{8,9},{9,10},{10,1... | collective-permute-start | bytes 1572872 | tf_op jit(solution)/shard_map/while/body/eval_jaxpr/ppermute | solution.py:23
  150.4 3.1 collective-permute-done
  153.5 2.8 convolution_dynamic-update-slice_fusion.2
  158.2 12.6 %collective-permute-start = (bf16[32,64,128]{2,1,0:T(8,128)(2,1)}, bf16[32,64,128]{2,1,0:T(8,128)(2,1)}, u32[]{:S(2)}, u32[]{:S(2)}) collective-permute-start(bf16[32,64,128]{2,1,0:T(8,128)(2,1)} %get-tuple-element.241), channel_id=1, source_target_pairs={{0,1},{1,2},{2,3},{3,4},{4,5},{5,6},{6,7},{7,8},{8,9},{9,10},{10,1... | collective-permute-start | bytes 1572872 | tf_op jit(solution)/shard_map/while/body/eval_jaxpr/ppermute | solution.py:23
  170.8 3.0 collective-permute-done
  173.8 2.8 convolution_dynamic-update-slice_fusion.2
  178.5 12.6 %collective-permute-start = (bf16[32,64,128]{2,1,0:T(8,128)(2,1)}, bf16[32,64,128]{2,1,0:T(8,128)(2,1)}, u32[]{:S(2)}, u32[]{:S(2)}) collective-permute-start(bf16[32,64,128]{2,1,0:T(8,128)(2,1)} %get-tuple-element.241), channel_id=1, source_target_pairs={{0,1},{1,2},{2,3},{3,4},{4,5},{5,6},{6,7},{7,8},{8,9},{9,10},{10,1... | collective-permute-start | bytes 1572872 | tf_op jit(solution)/shard_map/while/body/eval_jaxpr/ppermute | solution.py:23
  191.1 8.7 %collective-permute-done = bf16[32,64,128]{2,1,0:T(8,128)(2,1)} collective-permute-done((bf16[32,64,128]{2,1,0:T(8,128)(2,1)}, bf16[32,64,128]{2,1,0:T(8,128)(2,1)}, u32[]{:S(2)}, u32[]{:S(2)}) %collective-permute-start) | collective-permute-done | bytes 524320 | tf_op jit(solution)/shard_map/while/body/eval_jaxpr/ppermute | solution.py:23
  204.4 7.0 %collective-permute-start = (bf16[32,64,128]{2,1,0:T(8,128)(2,1)}, bf16[32,64,128]{2,1,0:T(8,128)(2,1)}, u32[]{:S(2)}, u32[]{:S(2)}) collective-permute-start(bf16[32,64,128]{2,1,0:T(8,128)(2,1)} %get-tuple-element.241), channel_id=1, source_target_pairs={{0,1},{1,2},{2,3},{3,4},{4,5},{5,6},{6,7},{7,8},{8,9},{9,10},{10,1... | collective-permute-start | bytes 1572872 | tf_op jit(solution)/shard_map/while/body/eval_jaxpr/ppermute | solution.py:23
  211.5 12.9 %collective-permute-done = bf16[32,64,128]{2,1,0:T(8,128)(2,1)} collective-permute-done((bf16[32,64,128]{2,1,0:T(8,128)(2,1)}, bf16[32,64,128]{2,1,0:T(8,128)(2,1)}, u32[]{:S(2)}, u32[]{:S(2)}) %collective-permute-start) | collective-permute-done | bytes 524320 | tf_op jit(solution)/shard_map/while/body/eval_jaxpr/ppermute | solution.py:23
  224.4 2.8 convolution_dynamic-update-slice_fusion.2
  229.1 3.6 collective-permute-start
  232.7 12.1 %collective-permute-done = bf16[32,64,128]{2,1,0:T(8,128)(2,1)} collective-permute-done((bf16[32,64,128]{2,1,0:T(8,128)(2,1)}, bf16[32,64,128]{2,1,0:T(8,128)(2,1)}, u32[]{:S(2)}, u32[]{:S(2)}) %collective-permute-start) | collective-permute-done | bytes 524320 | tf_op jit(solution)/shard_map/while/body/eval_jaxpr/ppermute | solution.py:23
  249.5 8.2 %collective-permute-start = (bf16[32,64,128]{2,1,0:T(8,128)(2,1)}, bf16[32,64,128]{2,1,0:T(8,128)(2,1)}, u32[]{:S(2)}, u32[]{:S(2)}) collective-permute-start(bf16[32,64,128]{2,1,0:T(8,128)(2,1)} %get-tuple-element.241), channel_id=1, source_target_pairs={{0,1},{1,2},{2,3},{3,4},{4,5},{5,6},{6,7},{7,8},{8,9},{9,10},{10,1... | collective-permute-start | bytes 1572872 | tf_op jit(solution)/shard_map/while/body/eval_jaxpr/ppermute | solution.py:23
  257.7 7.4 %collective-permute-done = bf16[32,64,128]{2,1,0:T(8,128)(2,1)} collective-permute-done((bf16[32,64,128]{2,1,0:T(8,128)(2,1)}, bf16[32,64,128]{2,1,0:T(8,128)(2,1)}, u32[]{:S(2)}, u32[]{:S(2)}) %collective-permute-start) | collective-permute-done | bytes 524320 | tf_op jit(solution)/shard_map/while/body/eval_jaxpr/ppermute | solution.py:23
  265.1 2.8 convolution_dynamic-update-slice_fusion.2
  269.7 12.3 %collective-permute-start = (bf16[32,64,128]{2,1,0:T(8,128)(2,1)}, bf16[32,64,128]{2,1,0:T(8,128)(2,1)}, u32[]{:S(2)}, u32[]{:S(2)}) collective-permute-start(bf16[32,64,128]{2,1,0:T(8,128)(2,1)} %get-tuple-element.241), channel_id=1, source_target_pairs={{0,1},{1,2},{2,3},{3,4},{4,5},{5,6},{6,7},{7,8},{8,9},{9,10},{10,1... | collective-permute-start | bytes 1572872 | tf_op jit(solution)/shard_map/while/body/eval_jaxpr/ppermute | solution.py:23
  282.1 6.3 collective-permute-done
  293.0 12.0 %collective-permute-start = (bf16[32,64,128]{2,1,0:T(8,128)(2,1)}, bf16[32,64,128]{2,1,0:T(8,128)(2,1)}, u32[]{:S(2)}, u32[]{:S(2)}) collective-permute-start(bf16[32,64,128]{2,1,0:T(8,128)(2,1)} %get-tuple-element.241), channel_id=1, source_target_pairs={{0,1},{1,2},{2,3},{3,4},{4,5},{5,6},{6,7},{7,8},{8,9},{9,10},{10,1... | collective-permute-start | bytes 1572872 | tf_op jit(solution)/shard_map/while/body/eval_jaxpr/ppermute | solution.py:23
  305.1 8.4 %collective-permute-done = bf16[32,64,128]{2,1,0:T(8,128)(2,1)} collective-permute-done((bf16[32,64,128]{2,1,0:T(8,128)(2,1)}, bf16[32,64,128]{2,1,0:T(8,128)(2,1)}, u32[]{:S(2)}, u32[]{:S(2)}) %collective-permute-start) | collective-permute-done | bytes 524320 | tf_op jit(solution)/shard_map/while/body/eval_jaxpr/ppermute | solution.py:23
  313.5 2.8 convolution_dynamic-update-slice_fusion.2
  318.1 11.2 %collective-permute-start = (bf16[32,64,128]{2,1,0:T(8,128)(2,1)}, bf16[32,64,128]{2,1,0:T(8,128)(2,1)}, u32[]{:S(2)}, u32[]{:S(2)}) collective-permute-start(bf16[32,64,128]{2,1,0:T(8,128)(2,1)} %get-tuple-element.241), channel_id=1, source_target_pairs={{0,1},{1,2},{2,3},{3,4},{4,5},{5,6},{6,7},{7,8},{8,9},{9,10},{10,1... | collective-permute-start | bytes 1572872 | tf_op jit(solution)/shard_map/while/body/eval_jaxpr/ppermute | solution.py:23
  329.4 9.7 %collective-permute-done = bf16[32,64,128]{2,1,0:T(8,128)(2,1)} collective-permute-done((bf16[32,64,128]{2,1,0:T(8,128)(2,1)}, bf16[32,64,128]{2,1,0:T(8,128)(2,1)}, u32[]{:S(2)}, u32[]{:S(2)}) %collective-permute-start) | collective-permute-done | bytes 524320 | tf_op jit(solution)/shard_map/while/body/eval_jaxpr/ppermute | solution.py:23
  343.7 9.7 %collective-permute-start = (bf16[32,64,128]{2,1,0:T(8,128)(2,1)}, bf16[32,64,128]{2,1,0:T(8,128)(2,1)}, u32[]{:S(2)}, u32[]{:S(2)}) collective-permute-start(bf16[32,64,128]{2,1,0:T(8,128)(2,1)} %get-tuple-element.241), channel_id=1, source_target_pairs={{0,1},{1,2},{2,3},{3,4},{4,5},{5,6},{6,7},{7,8},{8,9},{9,10},{10,1... | collective-permute-start | bytes 1572872 | tf_op jit(solution)/shard_map/while/body/eval_jaxpr/ppermute | solution.py:23
  353.4 9.8 %collective-permute-done = bf16[32,64,128]{2,1,0:T(8,128)(2,1)} collective-permute-done((bf16[32,64,128]{2,1,0:T(8,128)(2,1)}, bf16[32,64,128]{2,1,0:T(8,128)(2,1)}, u32[]{:S(2)}, u32[]{:S(2)}) %collective-permute-start) | collective-permute-done | bytes 524320 | tf_op jit(solution)/shard_map/while/body/eval_jaxpr/ppermute | solution.py:23
  363.2 2.8 convolution_dynamic-update-slice_fusion.2
  367.9 10.5 %collective-permute-start = (bf16[32,64,128]{2,1,0:T(8,128)(2,1)}, bf16[32,64,128]{2,1,0:T(8,128)(2,1)}, u32[]{:S(2)}, u32[]{:S(2)}) collective-permute-start(bf16[32,64,128]{2,1,0:T(8,128)(2,1)} %get-tuple-element.241), channel_id=1, source_target_pairs={{0,1},{1,2},{2,3},{3,4},{4,5},{5,6},{6,7},{7,8},{8,9},{9,10},{10,1... | collective-permute-start | bytes 1572872 | tf_op jit(solution)/shard_map/while/body/eval_jaxpr/ppermute | solution.py:23
  378.5 8.1 %collective-permute-done = bf16[32,64,128]{2,1,0:T(8,128)(2,1)} collective-permute-done((bf16[32,64,128]{2,1,0:T(8,128)(2,1)}, bf16[32,64,128]{2,1,0:T(8,128)(2,1)}, u32[]{:S(2)}, u32[]{:S(2)}) %collective-permute-start) | collective-permute-done | bytes 524320 | tf_op jit(solution)/shard_map/while/body/eval_jaxpr/ppermute | solution.py:23
  392.0 3.0 copy.106
  396.9 229.4 %all-gather.3.cloned.1.call-done = f32[16384,96]{1,0:T(8,128)} async-done(((f32[512,96]{1,0:T(8,128)}), f32[16384,96]{1,0:T(8,128)}) %all-gather.3.cloned.1.call-update) | async-done | bytes 6291472 | tf_op jit(solution)/shard_map/all_gather | solution.py:99
  626.2 4.0 reduce_sum.49
  (78 shorter events, 67.6 us)
Async XLA Ops:
  7.2 11.7 %copy-start.7 = (bf16[32,64,128]{2,1,0:T(8,128)(2,1)S(1)}, bf16[32,64,128]{2,1,0:T(8,128)(2,1)}, u32[]{:S(2)}) copy-start(bf16[32,64,128]{2,1,0:T(8,128)(2,1)} %param.10) | copy-start | bytes 1572868
  7.2 619.0 %all-gather.3.cloned.1.call-start = ((), (), s32[]{:S(2)}) async-start(), calls=%async_computation | async-start | bytes 8650752 | tf_op jit(solution)/shard_map/all_gather | solution.py:99
  8.3 12.2 %copy-start.8 = (bf16[32,64,128]{2,1,0:T(8,128)(2,1)}, bf16[32,64,128]{2,1,0:T(8,128)(2,1)S(1)}, u32[]{:S(2)}) copy-start(bf16[32,64,128]{2,1,0:T(8,128)(2,1)S(1)} %copy.133) | copy-start | bytes 1572868
  12.3 10.8 %collective-permute-start.2 = (bf16[33,64,2]{1,2,0:T(2,128)(2,1)S(1)}, bf16[33,64,2]{1,2,0:T(2,128)(2,1)S(1)}, u32[]{:S(2)}, u32[]{:S(2)}) collective-permute-start(bf16[33,64,2]{1,2,0:T(2,128)(2,1)S(1)} %copy.110), channel_id=1, source_target_pairs={{16,0},{32,16},{48,32},{64,48},{80,64},{96,80},{112,96},{128,112},... | collective-permute-start | bytes 25352 | tf_op jit(solution)/shard_map/ppermute | solution.py:15
  13.9 9.2 %collective-permute-start.1 = (bf16[33,64,2]{1,2,0:T(2,128)(2,1)S(1)}, bf16[33,64,2]{1,2,0:T(2,128)(2,1)S(1)}, u32[]{:S(2)}, u32[]{:S(2)}) collective-permute-start(bf16[33,64,2]{1,2,0:T(2,128)(2,1)S(1)} %copy.109), channel_id=1, source_target_pairs={{0,16},{16,32},{32,48},{48,64},{64,80},{80,96},{96,112},{112,128},... | collective-permute-start | bytes 25352 | tf_op jit(solution)/shard_map/ppermute | solution.py:14
  32.3 2.2 copy-start
  32.3 2.4 copy-start.2
  34.6 1.3 copy-start.4
  46.0 4.3 copy-start.1
  46.0 4.3 copy-start.3
  46.0 4.3 copy-start.5
  55.8 16.7 %collective-permute-start = (bf16[32,64,128]{2,1,0:T(8,128)(2,1)}, bf16[32,64,128]{2,1,0:T(8,128)(2,1)}, u32[]{:S(2)}, u32[]{:S(2)}) collective-permute-start(bf16[32,64,128]{2,1,0:T(8,128)(2,1)} %get-tuple-element.241), channel_id=1, source_target_pairs={{0,1},{1,2},{2,3},{3,4},{4,5},{5,6},{6,7},{7,8},{8,9},{9,10},{10,1... | collective-permute-start | bytes 1572872 | tf_op jit(solution)/shard_map/while/body/eval_jaxpr/ppermute | solution.py:23
  77.1 15.6 %collective-permute-start = (bf16[32,64,128]{2,1,0:T(8,128)(2,1)}, bf16[32,64,128]{2,1,0:T(8,128)(2,1)}, u32[]{:S(2)}, u32[]{:S(2)}) collective-permute-start(bf16[32,64,128]{2,1,0:T(8,128)(2,1)} %get-tuple-element.241), channel_id=1, source_target_pairs={{0,1},{1,2},{2,3},{3,4},{4,5},{5,6},{6,7},{7,8},{8,9},{9,10},{10,1... | collective-permute-start | bytes 1572872 | tf_op jit(solution)/shard_map/while/body/eval_jaxpr/ppermute | solution.py:23
  97.4 15.6 %collective-permute-start = (bf16[32,64,128]{2,1,0:T(8,128)(2,1)}, bf16[32,64,128]{2,1,0:T(8,128)(2,1)}, u32[]{:S(2)}, u32[]{:S(2)}) collective-permute-start(bf16[32,64,128]{2,1,0:T(8,128)(2,1)} %get-tuple-element.241), channel_id=1, source_target_pairs={{0,1},{1,2},{2,3},{3,4},{4,5},{5,6},{6,7},{7,8},{8,9},{9,10},{10,1... | collective-permute-start | bytes 1572872 | tf_op jit(solution)/shard_map/while/body/eval_jaxpr/ppermute | solution.py:23
  117.7 15.6 %collective-permute-start = (bf16[32,64,128]{2,1,0:T(8,128)(2,1)}, bf16[32,64,128]{2,1,0:T(8,128)(2,1)}, u32[]{:S(2)}, u32[]{:S(2)}) collective-permute-start(bf16[32,64,128]{2,1,0:T(8,128)(2,1)} %get-tuple-element.241), channel_id=1, source_target_pairs={{0,1},{1,2},{2,3},{3,4},{4,5},{5,6},{6,7},{7,8},{8,9},{9,10},{10,1... | collective-permute-start | bytes 1572872 | tf_op jit(solution)/shard_map/while/body/eval_jaxpr/ppermute | solution.py:23
  137.9 15.6 %collective-permute-start = (bf16[32,64,128]{2,1,0:T(8,128)(2,1)}, bf16[32,64,128]{2,1,0:T(8,128)(2,1)}, u32[]{:S(2)}, u32[]{:S(2)}) collective-permute-start(bf16[32,64,128]{2,1,0:T(8,128)(2,1)} %get-tuple-element.241), channel_id=1, source_target_pairs={{0,1},{1,2},{2,3},{3,4},{4,5},{5,6},{6,7},{7,8},{8,9},{9,10},{10,1... | collective-permute-start | bytes 1572872 | tf_op jit(solution)/shard_map/while/body/eval_jaxpr/ppermute | solution.py:23
  158.2 15.6 %collective-permute-start = (bf16[32,64,128]{2,1,0:T(8,128)(2,1)}, bf16[32,64,128]{2,1,0:T(8,128)(2,1)}, u32[]{:S(2)}, u32[]{:S(2)}) collective-permute-start(bf16[32,64,128]{2,1,0:T(8,128)(2,1)} %get-tuple-element.241), channel_id=1, source_target_pairs={{0,1},{1,2},{2,3},{3,4},{4,5},{5,6},{6,7},{7,8},{8,9},{9,10},{10,1... | collective-permute-start | bytes 1572872 | tf_op jit(solution)/shard_map/while/body/eval_jaxpr/ppermute | solution.py:23
  178.5 21.3 %collective-permute-start = (bf16[32,64,128]{2,1,0:T(8,128)(2,1)}, bf16[32,64,128]{2,1,0:T(8,128)(2,1)}, u32[]{:S(2)}, u32[]{:S(2)}) collective-permute-start(bf16[32,64,128]{2,1,0:T(8,128)(2,1)} %get-tuple-element.241), channel_id=1, source_target_pairs={{0,1},{1,2},{2,3},{3,4},{4,5},{5,6},{6,7},{7,8},{8,9},{9,10},{10,1... | collective-permute-start | bytes 1572872 | tf_op jit(solution)/shard_map/while/body/eval_jaxpr/ppermute | solution.py:23
  204.4 20.0 %collective-permute-start = (bf16[32,64,128]{2,1,0:T(8,128)(2,1)}, bf16[32,64,128]{2,1,0:T(8,128)(2,1)}, u32[]{:S(2)}, u32[]{:S(2)}) collective-permute-start(bf16[32,64,128]{2,1,0:T(8,128)(2,1)} %get-tuple-element.241), channel_id=1, source_target_pairs={{0,1},{1,2},{2,3},{3,4},{4,5},{5,6},{6,7},{7,8},{8,9},{9,10},{10,1... | collective-permute-start | bytes 1572872 | tf_op jit(solution)/shard_map/while/body/eval_jaxpr/ppermute | solution.py:23
  229.1 15.7 %collective-permute-start = (bf16[32,64,128]{2,1,0:T(8,128)(2,1)}, bf16[32,64,128]{2,1,0:T(8,128)(2,1)}, u32[]{:S(2)}, u32[]{:S(2)}) collective-permute-start(bf16[32,64,128]{2,1,0:T(8,128)(2,1)} %get-tuple-element.241), channel_id=1, source_target_pairs={{0,1},{1,2},{2,3},{3,4},{4,5},{5,6},{6,7},{7,8},{8,9},{9,10},{10,1... | collective-permute-start | bytes 1572872 | tf_op jit(solution)/shard_map/while/body/eval_jaxpr/ppermute | solution.py:23
  249.5 15.6 %collective-permute-start = (bf16[32,64,128]{2,1,0:T(8,128)(2,1)}, bf16[32,64,128]{2,1,0:T(8,128)(2,1)}, u32[]{:S(2)}, u32[]{:S(2)}) collective-permute-start(bf16[32,64,128]{2,1,0:T(8,128)(2,1)} %get-tuple-element.241), channel_id=1, source_target_pairs={{0,1},{1,2},{2,3},{3,4},{4,5},{5,6},{6,7},{7,8},{8,9},{9,10},{10,1... | collective-permute-start | bytes 1572872 | tf_op jit(solution)/shard_map/while/body/eval_jaxpr/ppermute | solution.py:23
  269.7 18.6 %collective-permute-start = (bf16[32,64,128]{2,1,0:T(8,128)(2,1)}, bf16[32,64,128]{2,1,0:T(8,128)(2,1)}, u32[]{:S(2)}, u32[]{:S(2)}) collective-permute-start(bf16[32,64,128]{2,1,0:T(8,128)(2,1)} %get-tuple-element.241), channel_id=1, source_target_pairs={{0,1},{1,2},{2,3},{3,4},{4,5},{5,6},{6,7},{7,8},{8,9},{9,10},{10,1... | collective-permute-start | bytes 1572872 | tf_op jit(solution)/shard_map/while/body/eval_jaxpr/ppermute | solution.py:23
  293.0 20.5 %collective-permute-start = (bf16[32,64,128]{2,1,0:T(8,128)(2,1)}, bf16[32,64,128]{2,1,0:T(8,128)(2,1)}, u32[]{:S(2)}, u32[]{:S(2)}) collective-permute-start(bf16[32,64,128]{2,1,0:T(8,128)(2,1)} %get-tuple-element.241), channel_id=1, source_target_pairs={{0,1},{1,2},{2,3},{3,4},{4,5},{5,6},{6,7},{7,8},{8,9},{9,10},{10,1... | collective-permute-start | bytes 1572872 | tf_op jit(solution)/shard_map/while/body/eval_jaxpr/ppermute | solution.py:23
  318.1 21.0 %collective-permute-start = (bf16[32,64,128]{2,1,0:T(8,128)(2,1)}, bf16[32,64,128]{2,1,0:T(8,128)(2,1)}, u32[]{:S(2)}, u32[]{:S(2)}) collective-permute-start(bf16[32,64,128]{2,1,0:T(8,128)(2,1)} %get-tuple-element.241), channel_id=1, source_target_pairs={{0,1},{1,2},{2,3},{3,4},{4,5},{5,6},{6,7},{7,8},{8,9},{9,10},{10,1... | collective-permute-start | bytes 1572872 | tf_op jit(solution)/shard_map/while/body/eval_jaxpr/ppermute | solution.py:23
  343.7 19.5 %collective-permute-start = (bf16[32,64,128]{2,1,0:T(8,128)(2,1)}, bf16[32,64,128]{2,1,0:T(8,128)(2,1)}, u32[]{:S(2)}, u32[]{:S(2)}) collective-permute-start(bf16[32,64,128]{2,1,0:T(8,128)(2,1)} %get-tuple-element.241), channel_id=1, source_target_pairs={{0,1},{1,2},{2,3},{3,4},{4,5},{5,6},{6,7},{7,8},{8,9},{9,10},{10,1... | collective-permute-start | bytes 1572872 | tf_op jit(solution)/shard_map/while/body/eval_jaxpr/ppermute | solution.py:23
  367.9 18.6 %collective-permute-start = (bf16[32,64,128]{2,1,0:T(8,128)(2,1)}, bf16[32,64,128]{2,1,0:T(8,128)(2,1)}, u32[]{:S(2)}, u32[]{:S(2)}) collective-permute-start(bf16[32,64,128]{2,1,0:T(8,128)(2,1)} %get-tuple-element.241), channel_id=1, source_target_pairs={{0,1},{1,2},{2,3},{3,4},{4,5},{5,6},{6,7},{7,8},{8,9},{9,10},{10,1... | collective-permute-start | bytes 1572872 | tf_op jit(solution)/shard_map/while/body/eval_jaxpr/ppermute | solution.py:23
  391.2 0.7 copy-start.9
  391.2 3.8 copy-start.6
Sparse Core Ops, SparseCore 0:
  392.1 234.0 all-gather.2
